TPU v7x, 32 devices: a whole 2x2x4 slice. The times are simulated.
32 devices in a mesh: grp: 2 (over y), row: 8 (over z, x), tile: 2 (over core).
Axes of the slice: x: 2, y: 2, z: 4, core: 2. Of those that a mesh axis runs over, the one named last changes fastest.
Arguments:
- right_side: bfloat16 [16, 4096, 384], P(('grp', 'row'), 'tile'), parts along dimension 0, may hold values from -6 to 6
- diag_inverse: bfloat16 [3, 4096, 4096], P(None, ('row', 'tile')), may hold values from -0.09375 to 0.09375
- u_factor: bfloat16 [8, 3, 4096, 384], P('row', None, 'tile'), may hold values from -0.5 to 0.5
- v_factor: bfloat16 [8, 3, 4096, 384], P('row', None, 'tile'), may hold values from -0.09375 to 0.09375
- ranks: int32 [8, 3], P('row'), may hold values from 64 to 384, as said below
- pivots: int32 [3], replicated, may hold values from 0 to 7, as said below
Outputs:
- solution: bfloat16 [3, 8192, 384], P(None, ('grp', 'row', 'tile')), parts along dimension 1
- residual_out: float32 [16, 4096, 384], P(('grp', 'row'), 'tile'), parts along dimension 0
There are 2 independent parts, one for each index of `grp`. A program takes and returns all parts, laid end to end along the dimension named above; an argument that names none is the same for every part. Nothing has to cross between parts.
Inputs may be any that keep to these rules, and one draw needn't show every extreme that they name: `ranks`: each entry is 384 // 6 times one of 1, 2, 3, 4, 6; in every draw some block row has rank 384 in every pivot column. `pivots`: distinct block rows of the strip; the first and the last block row are always among them, in an order drawn from the seed.
All inputs are finite; a program needn't handle non-finite values.
Results may differ from a plain program's by a relative error of at most 0.0085.
Values may be sent and summed in bfloat16 or wider, within the bound.
A program may use at most 64 MiB of HBM per device.

v0:
```python
import jax
import jax.numpy as jnp
from jax import lax
from jax.sharding import PartitionSpec as P

PIVOTS = 3


def spread(block, axis, holder):
    block = jnp.where(lax.axis_index(axis) == holder, block, jnp.zeros_like(block))
    return lax.psum(block, axis)


def local(right_side, diag_inverse, u_factor, v_factor, ranks, pivots):
    residual = right_side[0].astype(jnp.float32)
    half_rows = residual.shape[0]
    rank_width = u_factor.shape[3]
    columns = lax.broadcasted_iota(jnp.int32, (rank_width, 1), 0)
    my_block = lax.axis_index("row")
    tile_at = lax.axis_index("tile")
    solved_list = []
    for step in range(PIVOTS):
        root_block = pivots[step]
        current = residual.astype(jnp.bfloat16)
        half_pivot = spread(current, "row", root_block)
        whole_pivot = lax.all_gather(half_pivot, "tile", axis=0, tiled=True)
        part_unknowns = jnp.dot(
            diag_inverse[step], whole_pivot, preferred_element_type=jnp.float32
        ).astype(jnp.bfloat16)
        solved_list.append(part_unknowns)
        full_unknowns = lax.all_gather(part_unknowns, ("row", "tile"), axis=0, tiled=True)
        own_unknowns = lax.dynamic_slice_in_dim(full_unknowns, tile_at * half_rows, half_rows, 0)
        partial_value = lax.dot_general(
            v_factor[0, step],
            own_unknowns,
            (((0,), (0,)), ((), ())),
            preferred_element_type=jnp.float32,
        )
        coef = lax.psum(partial_value, "tile")
        coef = jnp.where(columns < ranks[0, step], coef, jnp.float32(0.0)).astype(jnp.bfloat16)
        update = jnp.dot(u_factor[0, step], coef, preferred_element_type=jnp.float32)
        finished = jnp.any(pivots[: step + 1] == my_block)
        residual = residual - jnp.where(finished, jnp.float32(0.0), update)
    return (jnp.stack(solved_list), residual[None])


def solution(mesh):
    in_specs = (
        P(("grp", "row"), "tile", None),
        P(None, ("row", "tile"), None),
        P("row", None, "tile", None),
        P("row", None, "tile", None),
        P("row", None),
        P(),
    )
    out_specs = (P(None, ("grp", "row", "tile"), None), P(("grp", "row"), "tile", None))
    return jax.shard_map(local, mesh=mesh, in_specs=in_specs, out_specs=out_specs, check_vma=False)
```

profile of v0, /device:TPU:0, one launch (start us, length us, event | category | flops | bytes accessed | tf_op | source)
XLA Modules:
  0.0 526.5 jit_solution(12442495691585397024)
XLA Ops:
  7.2 0.0 all-reduce.7.cloned.1.call-start
  7.2 1.4 fusion.65
  9.3 2.7 select_bitcast_fusion
  12.1 0.0 all-reduce.7.cloned.1.call-update
  12.1 0.0 all-gather.7.cloned.1.call-start
  12.1 91.6 %all-reduce.7.cloned.1.call-done = bf16[2048,384]{1,0:T(8,128)(2,1)} async-done(((bf16[2048,384]{1,0:T(8,128)(2,1)}), bf16[2048,384]{1,0:T(8,128)(2,1)}) %all-reduce.7.cloned.1.call-update) | async-done | bytes 1572880 | tf_op jit(solution)/shard_map/psum | solution.py:11
  103.7 0.0 all-gather.7.cloned.1.call-update
  103.8 0.0 all-gather.9.cloned.1.call-start
  103.8 13.0 %all-gather.7.cloned.1.call-done = bf16[4096,384]{1,0:T(8,128)(2,1)} async-done(((bf16[2048,384]{1,0:T(8,128)(2,1)}), bf16[4096,384]{1,0:T(8,128)(2,1)}) %all-gather.7.cloned.1.call-update) | async-done | bytes 3145744 | tf_op jit(solution)/shard_map/all_gather | solution.py:26
  116.8 4.2 fusion.43
  121.1 0.0 all-gather.9.cloned.1.call-update
  121.1 0.0 all-reduce.9.cloned.1.call-start
  121.1 0.8 copy.8
  123.3 0.6 fusion.64
  123.9 0.6 iota_compare_fusion.2
  124.6 45.0 %all-gather.9.cloned.1.call-done = bf16[4096,384]{0,1:T(8,128)(2,1)} async-done(((bf16[256,384]{0,1:T(8,128)(2,1)}), bf16[4096,384]{0,1:T(8,128)(2,1)}) %all-gather.9.cloned.1.call-update) | async-done | bytes 3145744 | tf_op jit(solution)/shard_map/all_gather | solution.py:31
  169.6 2.9 fusion.28
  172.5 5.1 all-reduce.12
  177.6 4.8 convert_select_fusion.1
  182.5 0.0 all-gather.11.cloned.1.call-start
  182.5 87.3 %all-reduce.9.cloned.1.call-done = bf16[2048,384]{0,1:T(8,128)(2,1)} async-done(((bf16[2048,384]{0,1:T(8,128)(2,1)}), bf16[2048,384]{0,1:T(8,128)(2,1)}) %all-reduce.9.cloned.1.call-update) | async-done | bytes 1572880 | tf_op jit(solution)/shard_map/psum | solution.py:11
  269.8 0.0 all-gather.13.cloned.1.call-start
  269.9 12.9 %all-gather.11.cloned.1.call-done = bf16[4096,384]{0,1:T(8,128)(2,1)} async-done(((bf16[2048,384]{0,1:T(8,128)(2,1)}), bf16[4096,384]{0,1:T(8,128)(2,1)}) %all-gather.11.cloned.1.call-update) | async-done | bytes 3145744 | tf_op jit(solution)/shard_map/all_gather | solution.py:26
  282.7 4.2 fusion.46
  287.0 0.0 all-gather.13.cloned.1.call-update
  287.0 0.0 all-reduce.11.cloned.1.call-start
  287.6 0.6 iota_compare_fusion.1
  288.3 0.7 compare_reduce_fusion.1
  289.0 46.6 %all-gather.13.cloned.1.call-done = bf16[4096,384]{0,1:T(8,128)(2,1)} async-done(((bf16[256,384]{0,1:T(8,128)(2,1)}), bf16[4096,384]{0,1:T(8,128)(2,1)}) %all-gather.13.cloned.1.call-update) | async-done | bytes 3145744 | tf_op jit(solution)/shard_map/all_gather | solution.py:31
  335.5 2.9 fusion.33
  338.4 5.1 all-reduce.13
  343.5 5.3 %convert_select_fusion = (bf16[2048,384]{0,1:T(8,128)(2,1)}, f32[2048,384]{0,1:T(8,128)S(1)}) fusion(pred[]{:T(512)S(6)} %eq.31, f32[2048,384]{0,1:T(8,128)} %get-tuple-element.11, bf16[1,3,2048,384]{3,2,1,0:T(8,128)(2,1)} %param.8, bf16[384,384]{1,0:T(8,128)(2,1)S(1)} %all-reduce.13, pred[384]{0:T(512)(128)(4,1)S(1)} %iota_compare_fusion.1, ...), kind=kOutput, calls=%fused_computation.25 | convolution fusion | flops 607272960 | bytes 9732993 | tf_op jit(solution)/shard_map/dot_general | solution.py:41
  348.8 0.0 all-reduce.11.cloned.1.call-update
  348.9 0.0 all-gather.15.cloned.1.call-start
  348.9 87.3 %all-reduce.11.cloned.1.call-done = bf16[2048,384]{0,1:T(8,128)(2,1)} async-done(((bf16[2048,384]{0,1:T(8,128)(2,1)}), bf16[2048,384]{0,1:T(8,128)(2,1)}) %all-reduce.11.cloned.1.call-update) | async-done | bytes 1572880 | tf_op jit(solution)/shard_map/psum | solution.py:11
  436.2 0.0 all-gather.15.cloned.1.call-update
  436.2 0.0 all-gather.17.cloned.1.call-start
  436.3 13.0 %all-gather.15.cloned.1.call-done = bf16[4096,384]{0,1:T(8,128)(2,1)} async-done(((bf16[2048,384]{0,1:T(8,128)(2,1)}), bf16[4096,384]{0,1:T(8,128)(2,1)}) %all-gather.15.cloned.1.call-update) | async-done | bytes 3145744 | tf_op jit(solution)/shard_map/all_gather | solution.py:26
  449.3 4.2 fusion.49
  453.5 0.7 iota_compare_fusion
  454.2 0.6 compare_reduce_fusion
  454.8 1.8 pad_maximum_fusion
  456.6 2.1 copy.9
  458.8 43.3 %all-gather.17.cloned.1.call-done = bf16[4096,384]{0,1:T(8,128)(2,1)} async-done(((bf16[256,384]{0,1:T(8,128)(2,1)}), bf16[4096,384]{0,1:T(8,128)(2,1)}) %all-gather.17.cloned.1.call-update) | async-done | bytes 3145744 | tf_op jit(solution)/shard_map/all_gather | solution.py:31
  502.1 3.7 fusion.38
  505.8 5.8 %all-reduce.14 = bf16[384,384]{1,0:T(8,128)(2,1)S(1)} all-reduce(f32[384,384]{1,0:T(8,128)} %fusion.38), channel_id=1, replica_groups=mesh['grp'=2,'row'=8,'tile'=2] {'tile'}, use_global_device_ids=true, to_apply=%region_7.8 | all-reduce | flops 147456 | bytes 884736 | tf_op jit(solution)/shard_map/psum | solution.py:39
  511.6 4.7 fusion
  516.4 3.5 copy.10
  (13 shorter events, 0.1 us)
Async XLA Ops:
  7.2 96.6 %all-reduce.7.cloned.1.call-start = ((), (), s32[]{:S(2)}) async-start(), calls=%async_computation | async-start | bytes 3145728 | tf_op jit(solution)/shard_map/psum | solution.py:11
  12.1 104.7 %all-gather.7.cloned.1.call-start = ((), (), s32[]{:S(2)}) async-start(), calls=%async_computation.1 | async-start | bytes 4718592 | tf_op jit(solution)/shard_map/all_gather | solution.py:26
  103.7 17.4 %copy-start = (bf16[1,2048,384]{2,1,0:T(8,128)(2,1)S(1)}, bf16[1,2048,384]{2,1,0:T(8,128)(2,1)}, u32[]{:S(2)}) copy-start(bf16[1,2048,384]{2,1,0:T(8,128)(2,1)} %param.6) | copy-start | bytes 4718596
  103.8 65.9 %all-gather.9.cloned.1.call-start = ((), (), s32[]{:S(2)}) async-start(), calls=%async_computation.2 | async-start | bytes 3342336 | tf_op jit(solution)/shard_map/all_gather | solution.py:31
  121.1 2.2 copy-start.3
  121.1 148.7 %all-reduce.9.cloned.1.call-start = ((), (), s32[]{:S(2)}) async-start(), calls=%async_computation.3 | async-start | bytes 3145728 | tf_op jit(solution)/shard_map/psum | solution.py:11
  182.5 100.3 %all-gather.11.cloned.1.call-start = ((), (), s32[]{:S(2)}) async-start(), calls=%async_computation.4 | async-start | bytes 4718592 | tf_op jit(solution)/shard_map/all_gather | solution.py:26
  269.8 18.5 %copy-start.4 = (s32[3]{0:T(128)S(1)}, s32[3]{0:T(128)}, u32[]{:S(2)}) copy-start(s32[3]{0:T(128)} %param.11) | copy-start | bytes 40
  269.8 65.7 %all-gather.13.cloned.1.call-start = ((), (), s32[]{:S(2)}) async-start(), calls=%async_computation.5 | async-start | bytes 3342336 | tf_op jit(solution)/shard_map/all_gather | solution.py:31
  287.0 149.2 %all-reduce.11.cloned.1.call-start = ((), (), s32[]{:S(2)}) async-start(), calls=%async_computation.6 | async-start | bytes 3145728 | tf_op jit(solution)/shard_map/psum | solution.py:11
  348.9 100.4 %all-gather.15.cloned.1.call-start = ((), (), s32[]{:S(2)}) async-start(), calls=%async_computation.7 | async-start | bytes 4718592 | tf_op jit(solution)/shard_map/all_gather | solution.py:26
  436.2 18.6 %copy-start.1 = (bf16[384,256]{1,0:T(8,128)(2,1)S(1)}, bf16[384,256]{1,0:T(8,128)(2,1)}, u32[]{:S(2)}) copy-start(bf16[384,256]{1,0:T(8,128)(2,1)} %fusion.43) | copy-start | bytes 589828
  436.2 18.6 %copy-start.2 = (bf16[384,256]{1,0:T(8,128)(2,1)S(1)}, bf16[384,256]{1,0:T(8,128)(2,1)}, u32[]{:S(2)}) copy-start(bf16[384,256]{1,0:T(8,128)(2,1)} %fusion.46) | copy-start | bytes 589828
  436.2 65.8 %all-gather.17.cloned.1.call-start = ((), (), s32[]{:S(2)}) async-start(), calls=%async_computation.8 | async-start | bytes 3342336 | tf_op jit(solution)/shard_map/all_gather | solution.py:31
Sparse Core Ops, SparseCore 0:
  12.2 91.4 all-reduce.6
  105.3 11.4 all-gather.6
  121.2 48.3 all-gather.8
  182.6 87.1 all-reduce.8
  271.2 11.4 all-gather.10
  287.1 48.3 all-gather.12
  349.0 87.1 all-reduce.10
  437.7 11.4 all-gather.14
  453.7 48.3 all-gather.16
where the time goes:
time: 527 us; the launch traced here: 526 us
  waiting for transfers between devices  440 us (83%)
  matrix products  37.1 us (7%)
  between operations  16.7 us (3%)
  blocking collectives  16 us (3%)
  local copies, waits for them, and re-layouts  8.52 us (2%)
  other arithmetic  7.75 us (1%)
    psum x3, waiting for transfers between devices, spread(): return lax.psum(block, axis)  266 us
    all_gather x3, waiting for transfers between devices, local(): lax.all_gather(part_unknowns, ('row', 'tile'), axis=0, tiled=True)  135 us
    all_gather x3, waiting for transfers between devices, local(): whole_pivot = lax.all_gather(half_pivot, 'tile', axis=0, tiled=True)  38.8 us
    psum x3, blocking collectives, local(): coef = lax.psum(partial_value, 'tile')  16 us
    dot_general x3, matrix products, local(): jnp.dot(u_factor[0, step], coef, preferred_element_type=jnp.float32)  14.9 us
    dot_general x3, matrix products, local(): jnp.dot(diag_inverse[step], whole_pivot, preferred_element_type=jnp.float32)  12.7 us
  transfers between devices with their start and end apart: 9, of which 9 were waited for; matrix products, arithmetic and copies ran while one was open for 2% of the time, Pallas kernels for 0%

commit v1 on v0

v1 whole, which is shorter than its diff:
```python
import functools

import jax
import jax.numpy as jnp
from jax import lax
from jax.experimental import pallas as pl
from jax.experimental.pallas import tpu as pltpu
from jax.sharding import PartitionSpec as P

PIVOTS = 3
MESH = pl.DeviceIdType.MESH


class Place:
    def __init__(self, rows):
        self.rows = rows
        self.lanes = rows // 2
        self.grp = lax.axis_index("grp")
        self.row = lax.axis_index("row")
        self.tile = lax.axis_index("tile")
        self.side = lax.rem(self.row, 2)
        self.lane = lax.div(self.row, 2)

    def peer(self, offset):
        return lax.rem(self.lane + offset, self.lanes) * 2 + self.side

    def source(self, offset):
        return lax.rem(self.lane + self.lanes - offset, self.lanes) * 2 + self.side

    def across(self, row):
        return row + 1 - 2 * self.side

    def to(self, row, tile):
        return (self.grp, row, tile)


def greet(at):
    barrier = pltpu.get_barrier_semaphore()
    targets = [at.to(at.across(at.row), at.tile), at.to(at.row, 1 - at.tile)]
    targets += [at.to(at.peer(k), at.tile) for k in range(1, at.lanes)]
    for target in targets:
        pl.semaphore_signal(barrier, inc=1, device_id=target, device_id_type=MESH)
    pl.semaphore_wait(barrier, len(targets))


def gather_body(at, src, out_at, sends, recv_col, recv_side, recv_tile):
    lanes = at.lanes
    started = []

    def send(source, slot, sem, recv, target):
        copy = pltpu.make_async_remote_copy(
            src_ref=source, dst_ref=slot, send_sem=sem, recv_sem=recv,
            device_id=target, device_id_type=MESH)
        copy.start()
        started.append(copy)

    def arrived(slot, recv):
        pltpu.make_async_remote_copy(
            src_ref=slot, dst_ref=slot, send_sem=sends.at[0], recv_sem=recv,
            device_id=at.to(at.row, 1 - at.tile), device_id_type=MESH).wait_recv()

    mine = out_at(at.row, at.tile)
    side_row = at.across(at.row)
    count = 0
    for k in range(1, lanes):
        send(src, mine, sends.at[count], recv_col.at[k], at.to(at.peer(k), at.tile))
        count += 1
    send(src, mine, sends.at[count], recv_side.at[0], at.to(side_row, at.tile))
    send(src, mine, sends.at[count + 1], recv_tile.at[0], at.to(at.row, 1 - at.tile))
    count += 2
    mine[...] = src[...]
    for k in range(1, lanes):
        slot = out_at(at.source(k), at.tile)
        arrived(slot, recv_col.at[k])
        send(slot, slot, sends.at[count], recv_side.at[k], at.to(side_row, at.tile))
        send(slot, slot, sends.at[count + 1], recv_tile.at[k], at.to(at.row, 1 - at.tile))
        count += 2
    for k in range(lanes):
        slot = out_at(at.across(at.source(k)), at.tile)
        arrived(slot, recv_side.at[k])
        send(slot, slot, sends.at[count], recv_tile.at[lanes + k], at.to(at.row, 1 - at.tile))
        count += 1
    for k in range(lanes):
        arrived(out_at(at.source(k), 1 - at.tile), recv_tile.at[k])
        arrived(out_at(at.across(at.source(k)), 1 - at.tile), recv_tile.at[lanes + k])
    for copy in started:
        copy.wait_send()


def gather_sems(rows):
    lanes = rows // 2
    return [
        pltpu.SemaphoreType.DMA((4 * lanes,)),
        pltpu.SemaphoreType.DMA((lanes,)),
        pltpu.SemaphoreType.DMA((lanes,)),
        pltpu.SemaphoreType.DMA((rows,)),
    ]


def gather_kernel(rows, src, out, sends, recv_col, recv_side, recv_tile):
    at = Place(rows)
    greet(at)
    gather_body(at, src, lambda row, tile: out.at[row, tile], sends, recv_col, recv_side, recv_tile)


def spread_kernel(rows, flags, src, out, from_side, mixed, from_col, piece,
                  sends, recv_col, recv_side, recv_tile, rs_sends, rs_side, rs_col):
    at = Place(rows)
    lanes = at.lanes
    greet(at)
    side_row = at.across(at.row)
    order = list(range(1, lanes)) + [0]
    side_copies = {}
    for k in order:
        copy = pltpu.make_async_remote_copy(
            src_ref=src.at[at.across(at.peer(k))], dst_ref=from_side.at[k],
            send_sem=rs_sends.at[k], recv_sem=rs_side.at[k],
            device_id=at.to(side_row, at.tile), device_id_type=MESH)
        copy.start()
        side_copies[k] = copy
    own = flags[0]
    col_copies = {}
    for k in order:
        side_copies[k].wait_recv()
        value = src[at.peer(k)].astype(jnp.float32) * own
        value = value + from_side[k].astype(jnp.float32) * (1.0 - own)
        mixed[k] = value.astype(jnp.bfloat16)
        if k:
            copy = pltpu.make_async_remote_copy(
                src_ref=mixed.at[k], dst_ref=from_col.at[k],
                send_sem=rs_sends.at[lanes + k], recv_sem=rs_col.at[k],
                device_id=at.to(at.peer(k), at.tile), device_id_type=MESH)
            copy.start()
            col_copies[k] = copy
    total = mixed[0].astype(jnp.float32) * flags[1]
    for k in range(1, lanes):
        col_copies[k].wait_recv()
        total = total + from_col[k].astype(jnp.float32) * flags[1 + k]
    piece[...] = total.astype(jnp.bfloat16)
    for k in order:
        side_copies[k].wait_send()
        if k:
            col_copies[k].wait_send()
    gather_body(at, piece, lambda row, tile: out.at[tile, row], sends, recv_col, recv_side, recv_tile)


def spread(rows, tiles, current, root):
    half, width = current.shape
    part = half // rows
    lanes = rows // 2
    me = lax.axis_index("row")
    lane = me // 2
    sources = lax.rem(lane + lanes - jnp.arange(lanes, dtype=jnp.int32), lanes)
    flags = jnp.concatenate([(root == me)[None], sources == root // 2]).astype(jnp.float32)
    out = pl.pallas_call(
        functools.partial(spread_kernel, rows),
        out_shape=jax.ShapeDtypeStruct((tiles, rows, part, width), jnp.bfloat16),
        in_specs=[pl.BlockSpec(memory_space=pltpu.SMEM), pl.BlockSpec(memory_space=pltpu.VMEM)],
        out_specs=pl.BlockSpec(memory_space=pltpu.VMEM),
        scratch_shapes=[
            pltpu.VMEM((lanes, part, width), jnp.bfloat16),
            pltpu.VMEM((lanes, part, width), jnp.bfloat16),
            pltpu.VMEM((lanes, part, width), jnp.bfloat16),
            pltpu.VMEM((part, width), jnp.bfloat16),
        ] + gather_sems(rows) + [
            pltpu.SemaphoreType.DMA((2 * lanes,)),
            pltpu.SemaphoreType.DMA((lanes,)),
            pltpu.SemaphoreType.DMA((lanes,)),
        ],
        compiler_params=pltpu.CompilerParams(
            collective_id=0, has_side_effects=True, vmem_limit_bytes=32 * 1024 * 1024),
        name="spread",
    )(flags, current.reshape(rows, part, width))
    return out.reshape(tiles * half, width)


def gather(rows, tiles, block):
    part, width = block.shape
    return pl.pallas_call(
        functools.partial(gather_kernel, rows),
        out_shape=jax.ShapeDtypeStruct((rows, tiles, part, width), jnp.bfloat16),
        in_specs=[pl.BlockSpec(memory_space=pltpu.VMEM)],
        out_specs=pl.BlockSpec(memory_space=pltpu.VMEM),
        scratch_shapes=gather_sems(rows),
        compiler_params=pltpu.CompilerParams(
            collective_id=1, has_side_effects=True, vmem_limit_bytes=32 * 1024 * 1024),
        name="gather",
    )(block).reshape(rows * tiles * part, width)


def local(rows, tiles, right_side, diag_inverse, u_factor, v_factor, ranks, pivots):
    residual = right_side[0].astype(jnp.float32)
    half_rows = residual.shape[0]
    rank_width = u_factor.shape[3]
    columns = lax.broadcasted_iota(jnp.int32, (rank_width, 1), 0)
    my_block = lax.axis_index("row")
    tile_at = lax.axis_index("tile")
    solved_list = []
    for step in range(PIVOTS):
        current = residual.astype(jnp.bfloat16)
        whole_pivot = spread(rows, tiles, current, pivots[step])
        part_unknowns = jnp.dot(
            diag_inverse[step], whole_pivot, preferred_element_type=jnp.float32
        ).astype(jnp.bfloat16)
        solved_list.append(part_unknowns)
        full_unknowns = gather(rows, tiles, part_unknowns)
        own_unknowns = lax.dynamic_slice_in_dim(full_unknowns, tile_at * half_rows, half_rows, 0)
        partial_value = lax.dot_general(
            v_factor[0, step],
            own_unknowns,
            (((0,), (0,)), ((), ())),
            preferred_element_type=jnp.float32,
        )
        coef = lax.psum(partial_value, "tile")
        coef = jnp.where(columns < ranks[0, step], coef, jnp.float32(0.0)).astype(jnp.bfloat16)
        update = jnp.dot(u_factor[0, step], coef, preferred_element_type=jnp.float32)
        finished = jnp.any(pivots[: step + 1] == my_block)
        residual = residual - jnp.where(finished, jnp.float32(0.0), update)
    return (jnp.stack(solved_list), residual[None])


def solution(mesh):
    in_specs = (
        P(("grp", "row"), "tile", None),
        P(None, ("row", "tile"), None),
        P("row", None, "tile", None),
        P("row", None, "tile", None),
        P("row", None),
        P(),
    )
    out_specs = (P(None, ("grp", "row", "tile"), None), P(("grp", "row"), "tile", None))
    body = functools.partial(local, mesh.shape["row"], mesh.shape["tile"])
    return jax.shard_map(body, mesh=mesh, in_specs=in_specs, out_specs=out_specs, check_vma=False)
```

time: 527 us -> 343 us (0.65)
  waiting for transfers between devices: 440 us -> 0 us
  Pallas kernels: 0 us -> 265 us
  between operations: 16.7 us -> 10.6 us
    psum x3 -> x0, waiting for transfers between devices: 266 us -> none  [spread(): return lax.psum(block, axis)]
    pallas_call x0 -> x6, Pallas kernels: none -> 265 us  [the longest x3 166 us: spread(): pl.pallas_call(functools.partial(spread_kernel, rows), out_shape=jax.Shap...]
    all_gather x6 -> x0, waiting for transfers between devices: 174 us -> none  [the longest x3 135 us: local(): lax.all_gather(part_unknowns, ('row', 'tile'), axis=0, tiled=True)]
  transfers between devices with their start and end apart: 9 -> 0, of which waited for: 9 -> 0; matrix products, arithmetic and copies ran while one was open for 2% -> 0% of each run, Pallas kernels for 0% -> 0%
where the time goes in v1:
time: 343 us; the launch traced here: 341 us
  Pallas kernels  265 us (77%)
  matrix products  32.2 us (9%)
  blocking collectives  16.6 us (5%)
  local copies, waits for them, and re-layouts  10.7 us (3%)
  between operations  10.6 us (3%)
  other arithmetic  5.79 us (2%)
    pallas_call x3, Pallas kernels, spread(): pl.pallas_call(functools.partial(spread_kernel, rows), out_shape=jax.Shap...  166 us
    pallas_call x3, Pallas kernels, gather(): pl.pallas_call(functools.partial(gather_kernel, rows), out_shape=jax.Shap...  98.9 us
    psum x3, blocking collectives, local(): coef = lax.psum(partial_value, 'tile')  16.6 us
    dot_general x3, matrix products, local(): jnp.dot(u_factor[0, step], coef, preferred_element_type=jnp.float32)  15.3 us
    dot_general x3, matrix products, local(): jnp.dot(diag_inverse[step], whole_pivot, preferred_element_type=jnp.float32)  8.67 us
    dot_general x3, matrix products, local(): lax.dot_general(v_factor[0, step], own_unknowns, (((0,), (0,)), ((), ()))...  8.26 us

profile of v1, /device:TPU:0, one launch (start us, length us, event | category | flops | bytes accessed | tf_op | source)
XLA Modules:
  0.0 340.8 jit_solution(16844255561454750672)
XLA Ops:
  0.6 0.0 copy-start
  0.7 1.4 compare_reduce_fusion
  2.0 1.3 compare_reduce_fusion.1
  3.4 1.4 fusion.65
  4.7 0.6 iota_compare_fusion
  5.4 0.7 iota_compare_fusion.2
  6.0 0.6 iota_compare_fusion.1
  6.7 1.4 fusion.66
  17.9 0.1 add_convert_fusion.flags
  18.0 0.1 add_convert_fusion.2.flags
  18.0 0.1 add_convert_fusion.1.flags
  18.1 1.7 copy.9
  19.8 0.0 copy-done
  19.8 54.7 %spread.3 = bf16[2,8,256,384]{3,2,1,0:T(8,128)(2,1)S(1)} custom-call(f32[5]{0:T(128)S(1)} %add_convert_fusion.flags, bf16[8,256,384]{2,1,0:T(8,128)(2,1)S(1)} %bitcast.94), custom_call_target="tpu_custom_call" | custom-call | tf_op jit(solution)/shard_map/spread/pallas_call | solution.py:155
  74.5 2.9 fusion.43
  77.4 32.8 %gather.3 = bf16[8,2,256,384]{3,2,1,0:T(8,128)(2,1)S(1)} custom-call(bf16[256,384]{1,0:T(8,128)(2,1)S(1)} %bitcast.103), custom_call_target="tpu_custom_call" | custom-call | tf_op jit(solution)/shard_map/gather/pallas_call | solution.py:179
  110.2 2.4 fusion.28
  112.7 5.2 %all-reduce.3 = bf16[384,384]{1,0:T(8,128)(2,1)S(1)} all-reduce(f32[384,384]{1,0:T(8,128)S(1)} %fusion.28), channel_id=1, replica_groups=mesh['grp'=2,'row'=8,'tile'=2] {'tile'}, use_global_device_ids=true, to_apply=%region_0.1 | all-reduce | flops 147456 | bytes 884736 | tf_op jit(solution)/shard_map/psum | solution.py:214
  117.9 4.8 %fusion.67 = (bf16[2048,384]{0,1:T(8,128)(2,1)}, f32[2048,384]{0,1:T(8,128)}) fusion(bf16[1,3,2048,384]{3,2,1,0:T(8,128)(2,1)} %param.8, bf16[384,384]{1,0:T(8,128)(2,1)S(1)} %all-reduce.3, pred[384]{0:T(512)(128)(4,1)S(1)} %iota_compare_fusion.2, pred[]{:T(512)} %bitcast.11, bf16[1,2048,384]{1,2,0:T(8,128)(2,1)S(1)} %copy.9), kind=kOutput, calls=%fused_computation.69 | convolution fusion | flops 607272960 | bytes 8160128 | tf_op jit(solution)/shard_map/dot_general | solution.py:216
  122.7 1.9 copy.10
  124.5 55.7 %spread.4 = bf16[2,8,256,384]{3,2,1,0:T(8,128)(2,1)S(1)} custom-call(f32[5]{0:T(128)S(1)} %add_convert_fusion.1.flags, bf16[8,256,384]{2,1,0:T(8,128)(2,1)S(1)} %bitcast.95), custom_call_target="tpu_custom_call" | custom-call | tf_op jit(solution)/shard_map/spread/pallas_call | solution.py:155
  180.2 2.9 fusion.46
  183.1 33.1 %gather.4 = bf16[8,2,256,384]{3,2,1,0:T(8,128)(2,1)S(1)} custom-call(bf16[256,384]{1,0:T(8,128)(2,1)S(1)} %bitcast.105), custom_call_target="tpu_custom_call" | custom-call | tf_op jit(solution)/shard_map/gather/pallas_call | solution.py:179
  216.2 2.4 fusion.33
  218.6 5.4 %all-reduce.4 = bf16[384,384]{1,0:T(8,128)(2,1)S(1)} all-reduce(f32[384,384]{1,0:T(8,128)S(1)} %fusion.33), channel_id=1, replica_groups=mesh['grp'=2,'row'=8,'tile'=2] {'tile'}, use_global_device_ids=true, to_apply=%region_2.3 | all-reduce | flops 147456 | bytes 884736 | tf_op jit(solution)/shard_map/psum | solution.py:214
  224.0 5.8 %fusion.68 = (bf16[2048,384]{0,1:T(8,128)(2,1)S(1)}, f32[2048,384]{0,1:T(8,128)}) fusion(f32[2048,384]{0,1:T(8,128)} %get-tuple-element.11, bf16[1,3,2048,384]{3,2,1,0:T(8,128)(2,1)} %param.8, bf16[384,384]{1,0:T(8,128)(2,1)S(1)} %all-reduce.4, pred[384]{0:T(512)(128)(4,1)S(1)} %iota_compare_fusion.1, pred[]{:T(512)} %compare_reduce_fusion.1), kind=kOutput, calls=%fused_computation.70 | convolution fusion | flops 606486528 | bytes 9732992 | tf_op jit(solution)/shard_map/dot_general | solution.py:216
  229.8 0.9 copy.12
  230.7 55.7 %spread.5 = bf16[2,8,256,384]{3,2,1,0:T(8,128)(2,1)S(1)} custom-call(f32[5]{0:T(128)S(1)} %add_convert_fusion.2.flags, bf16[8,256,384]{2,1,0:T(8,128)(2,1)S(1)} %bitcast.96), custom_call_target="tpu_custom_call" | custom-call | tf_op jit(solution)/shard_map/spread/pallas_call | solution.py:155
  286.3 2.9 fusion.49
  289.2 0.9 pad_maximum_fusion
  290.1 33.0 %gather.5 = bf16[8,2,256,384]{3,2,1,0:T(8,128)(2,1)S(1)} custom-call(bf16[256,384]{1,0:T(8,128)(2,1)S(1)} %bitcast.108), custom_call_target="tpu_custom_call" | custom-call | tf_op jit(solution)/shard_map/gather/pallas_call | solution.py:179
  323.1 0.0 copy-start.1
  323.1 3.4 fusion.38
  326.5 6.0 %all-reduce.5 = bf16[384,384]{1,0:T(8,128)(2,1)S(1)} all-reduce(f32[384,384]{1,0:T(8,128)} %fusion.38), channel_id=1, replica_groups=mesh['grp'=2,'row'=8,'tile'=2] {'tile'}, use_global_device_ids=true, to_apply=%region_4.5 | all-reduce | flops 147456 | bytes 884736 | tf_op jit(solution)/shard_map/psum | solution.py:214
  332.5 0.0 copy-done.1
  332.5 4.8 %fusion = f32[1,2048,384]{1,2,0:T(8,128)} fusion(f32[2048,384]{0,1:T(8,128)S(1)} %copy-done.1, bf16[1,3,2048,384]{3,2,1,0:T(8,128)(2,1)} %param.8, pred[]{:T(512)} %compare_reduce_fusion, bf16[384,384]{1,0:T(8,128)(2,1)S(1)} %all-reduce.5, pred[384]{0:T(512)(128)(4,1)S(1)} %iota_compare_fusion), kind=kOutput, calls=%fused_computation.2 | convolution fusion | flops 605700096 | bytes 8160128 | tf_op jit(solution)/shard_map/dot_general | solution.py:216
  337.3 3.5 %copy.14 = f32[1,2048,384]{2,1,0:T(8,128)} copy(f32[1,2048,384]{1,2,0:T(8,128)} %fusion) | data formatting | bytes 6291456
  (2 shorter events, 0.0 us)
Async XLA Ops:
  0.6 19.2 %copy-start = (bf16[1,2048,384]{2,1,0:T(8,128)(2,1)S(1)}, bf16[1,2048,384]{2,1,0:T(8,128)(2,1)}, u32[]{:S(2)}) copy-start(bf16[1,2048,384]{2,1,0:T(8,128)(2,1)} %param.6) | copy-start | bytes 4718596
  323.1 9.4 %copy-start.1 = (f32[2048,384]{0,1:T(8,128)S(1)}, f32[2048,384]{0,1:T(8,128)}, u32[]{:S(2)}) copy-start(f32[2048,384]{0,1:T(8,128)} %get-tuple-element.13) | copy-start | bytes 9437188

commit v2 on v1

--- a/solution.py
+++ b/solution.py
@@ -43,68 +43,152 @@
     pl.semaphore_wait(barrier, len(targets))
 
 
-def gather_body(at, src, out_at, sends, recv_col, recv_side, recv_tile):
-    lanes = at.lanes
-    started = []
-
-    def send(source, slot, sem, recv, target):
-        copy = pltpu.make_async_remote_copy(
-            src_ref=source, dst_ref=slot, send_sem=sem, recv_sem=recv,
+def each(low, high, body):
+    def step(index, carry):
+        body(index)
+        return carry
+
+    lax.fori_loop(low, high, step, 0)
+
+
+def gather_body(at, cuts, src, out_at, sems):
+    z_right, z_left, z_recv, x_send, x_recv, t_send, t_recv = sems
+    lane, last = at.lane, at.lanes - 1
+    side_row = at.across(at.row)
+    mate = 1 - at.tile
+
+    def copy(source, slot, send_sem, recv_sem, target):
+        return pltpu.make_async_remote_copy(
+            src_ref=source, dst_ref=slot, send_sem=send_sem, recv_sem=recv_sem,
             device_id=target, device_id_type=MESH)
-        copy.start()
-        started.append(copy)
-
-    def arrived(slot, recv):
-        pltpu.make_async_remote_copy(
-            src_ref=slot, dst_ref=slot, send_sem=sends.at[0], recv_sem=recv,
-            device_id=at.to(at.row, 1 - at.tile), device_id_type=MESH).wait_recv()
-
-    mine = out_at(at.row, at.tile)
-    side_row = at.across(at.row)
-    count = 0
-    for k in range(1, lanes):
-        send(src, mine, sends.at[count], recv_col.at[k], at.to(at.peer(k), at.tile))
-        count += 1
-    send(src, mine, sends.at[count], recv_side.at[0], at.to(side_row, at.tile))
-    send(src, mine, sends.at[count + 1], recv_tile.at[0], at.to(at.row, 1 - at.tile))
-    count += 2
-    mine[...] = src[...]
-    for k in range(1, lanes):
-        slot = out_at(at.source(k), at.tile)
-        arrived(slot, recv_col.at[k])
-        send(slot, slot, sends.at[count], recv_side.at[k], at.to(side_row, at.tile))
-        send(slot, slot, sends.at[count + 1], recv_tile.at[k], at.to(at.row, 1 - at.tile))
-        count += 2
-    for k in range(lanes):
-        slot = out_at(at.across(at.source(k)), at.tile)
-        arrived(slot, recv_side.at[k])
-        send(slot, slot, sends.at[count], recv_tile.at[lanes + k], at.to(at.row, 1 - at.tile))
-        count += 1
-    for k in range(lanes):
-        arrived(out_at(at.source(k), 1 - at.tile), recv_tile.at[k])
-        arrived(out_at(at.across(at.source(k)), 1 - at.tile), recv_tile.at[lanes + k])
-    for copy in started:
-        copy.wait_send()
-
-
-def gather_sems(rows):
-    lanes = rows // 2
-    return [
-        pltpu.SemaphoreType.DMA((4 * lanes,)),
-        pltpu.SemaphoreType.DMA((lanes,)),
-        pltpu.SemaphoreType.DMA((lanes,)),
-        pltpu.SemaphoreType.DMA((rows,)),
-    ]
-
-
-def gather_kernel(rows, src, out, sends, recv_col, recv_side, recv_tile):
+
+    def right(source, owner, cut):
+        i = owner * cuts + cut
+        return copy(source, out_at(owner * 2 + at.side, at.tile, cut), z_right.at[i], z_recv.at[i],
+                    at.to(at.row + 2, at.tile))
+
+    def left(source, owner, cut):
+        i = owner * cuts + cut
+        return copy(source, out_at(owner * 2 + at.side, at.tile, cut), z_left.at[i], z_recv.at[i],
+                    at.to(at.row - 2, at.tile))
+
+    def sidewards(source, owner, cut):
+        i = owner * cuts + cut
+        return copy(source, out_at(owner * 2 + at.side, at.tile, cut), x_send.at[i], x_recv.at[i],
+                    at.to(side_row, at.tile))
+
+    def to_mate(source, row, cut):
+        i = row * cuts + cut
+        return copy(source, out_at(row, at.tile, cut), t_send.at[i], t_recv.at[i], at.to(at.row, mate))
+
+    def own_slot(owner, cut):
+        return out_at(owner * 2 + at.side, at.tile, cut)
+
+    def arrived(slot, sem):
+        copy(slot, slot, t_send.at[0], sem, at.to(at.row, mate)).wait_recv()
+
+    for cut in range(cuts):
+        @pl.when(lane < last)
+        def _(cut=cut):
+            right(src.at[cut], lane, cut).start()
+
+        @pl.when(lane > 0)
+        def _(cut=cut):
+            left(src.at[cut], lane, cut).start()
+
+        sidewards(src.at[cut], lane, cut).start()
+        to_mate(src.at[cut], at.row, cut).start()
+    for cut in range(cuts):
+        own_slot(lane, cut)[...] = src[cut]
+
+    def from_line(owner, cut):
+        slot = own_slot(owner, cut)
+        arrived(slot, z_recv.at[owner * cuts + cut])
+        return slot
+
+    def from_side(owner, cut):
+        row = owner * 2 + 1 - at.side
+        slot = out_at(row, at.tile, cut)
+        arrived(slot, x_recv.at[owner * cuts + cut])
+        to_mate(slot, row, cut).start()
+
+    def side_arrivals(k):
+        for cut in range(cuts):
+            @pl.when(lane >= k)
+            def _(cut=cut):
+                from_side(lane - k, cut)
+
+            @pl.when(jnp.logical_and(lane + k <= last, k > 0))
+            def _(cut=cut):
+                from_side(lane + k, cut)
+
+    def hop(k):
+        for cut in range(cuts):
+            @pl.when(lane >= k)
+            def _(cut=cut):
+                slot = from_line(lane - k, cut)
+
+                @pl.when(lane < last)
+                def _():
+                    right(slot, lane - k, cut).start()
+
+                sidewards(slot, lane - k, cut).start()
+                to_mate(slot, (lane - k) * 2 + at.side, cut).start()
+
+            @pl.when(lane + k <= last)
+            def _(cut=cut):
+                slot = from_line(lane + k, cut)
+
+                @pl.when(lane > 0)
+                def _():
+                    left(slot, lane + k, cut).start()
+
+                sidewards(slot, lane + k, cut).start()
+                to_mate(slot, (lane + k) * 2 + at.side, cut).start()
+        side_arrivals(k - 1)
+
+    each(1, at.lanes, hop)
+    side_arrivals(last)
+
+    def finish(owner):
+        for cut in range(cuts):
+            slot = own_slot(owner, cut)
+
+            @pl.when(jnp.logical_and(owner <= lane, lane < last))
+            def _(slot=slot, cut=cut):
+                right(slot, owner, cut).wait_send()
+
+            @pl.when(jnp.logical_and(owner >= lane, lane > 0))
+            def _(slot=slot, cut=cut):
+                left(slot, owner, cut).wait_send()
+
+            sidewards(slot, owner, cut).wait_send()
+            for side in range(2):
+                row = owner * 2 + side
+                arrived(out_at(row, mate, cut), t_recv.at[row * cuts + cut])
+                to_mate(out_at(row, at.tile, cut), row, cut).wait_send()
+
+    each(0, at.lanes, finish)
+
+
+def cuts_of(part):
+    return max(1, min(4, part // 16))
+
+
+def gather_sems(rows, cuts):
+    column = pltpu.SemaphoreType.DMA((rows // 2 * cuts,))
+    whole = pltpu.SemaphoreType.DMA((rows * cuts,))
+    return [column] * 5 + [whole] * 2
+
+
+def gather_kernel(rows, cuts, src, out, *sems):
     at = Place(rows)
     greet(at)
-    gather_body(at, src, lambda row, tile: out.at[row, tile], sends, recv_col, recv_side, recv_tile)
-
-
-def spread_kernel(rows, flags, src, out, from_side, mixed, from_col, piece,
-                  sends, recv_col, recv_side, recv_tile, rs_sends, rs_side, rs_col):
+    gather_body(at, cuts, src, lambda row, tile, cut: out.at[row, tile, cut], sems)
+
+
+def spread_kernel(rows, cuts, flags, src, out, from_side, mixed, from_col, piece,
+                  rs_sends, rs_side, rs_col, *sems):
     at = Place(rows)
     lanes = at.lanes
     greet(at)
@@ -136,37 +220,37 @@
     for k in range(1, lanes):
         col_copies[k].wait_recv()
         total = total + from_col[k].astype(jnp.float32) * flags[1 + k]
-    piece[...] = total.astype(jnp.bfloat16)
+    piece[...] = total.astype(jnp.bfloat16).reshape(piece.shape)
     for k in order:
         side_copies[k].wait_send()
         if k:
             col_copies[k].wait_send()
-    gather_body(at, piece, lambda row, tile: out.at[tile, row], sends, recv_col, recv_side, recv_tile)
+    gather_body(at, cuts, piece, lambda row, tile, cut: out.at[tile, row, cut], sems)
 
 
 def spread(rows, tiles, current, root):
     half, width = current.shape
     part = half // rows
     lanes = rows // 2
+    cuts = cuts_of(part)
     me = lax.axis_index("row")
     lane = me // 2
     sources = lax.rem(lane + lanes - jnp.arange(lanes, dtype=jnp.int32), lanes)
     flags = jnp.concatenate([(root == me)[None], sources == root // 2]).astype(jnp.float32)
     out = pl.pallas_call(
-        functools.partial(spread_kernel, rows),
-        out_shape=jax.ShapeDtypeStruct((tiles, rows, part, width), jnp.bfloat16),
+        functools.partial(spread_kernel, rows, cuts),
+        out_shape=jax.ShapeDtypeStruct((tiles, rows, cuts, part // cuts, width), jnp.bfloat16),
         in_specs=[pl.BlockSpec(memory_space=pltpu.SMEM), pl.BlockSpec(memory_space=pltpu.VMEM)],
         out_specs=pl.BlockSpec(memory_space=pltpu.VMEM),
         scratch_shapes=[
             pltpu.VMEM((lanes, part, width), jnp.bfloat16),
             pltpu.VMEM((lanes, part, width), jnp.bfloat16),
             pltpu.VMEM((lanes, part, width), jnp.bfloat16),
-            pltpu.VMEM((part, width), jnp.bfloat16),
-        ] + gather_sems(rows) + [
+            pltpu.VMEM((cuts, part // cuts, width), jnp.bfloat16),
             pltpu.SemaphoreType.DMA((2 * lanes,)),
             pltpu.SemaphoreType.DMA((lanes,)),
             pltpu.SemaphoreType.DMA((lanes,)),
-        ],
+        ] + gather_sems(rows, cuts),
         compiler_params=pltpu.CompilerParams(
             collective_id=0, has_side_effects=True, vmem_limit_bytes=32 * 1024 * 1024),
         name="spread",
@@ -176,16 +260,17 @@
 
 def gather(rows, tiles, block):
     part, width = block.shape
+    cuts = cuts_of(part)
     return pl.pallas_call(
-        functools.partial(gather_kernel, rows),
-        out_shape=jax.ShapeDtypeStruct((rows, tiles, part, width), jnp.bfloat16),
+        functools.partial(gather_kernel, rows, cuts),
+        out_shape=jax.ShapeDtypeStruct((rows, tiles, cuts, part // cuts, width), jnp.bfloat16),
         in_specs=[pl.BlockSpec(memory_space=pltpu.VMEM)],
         out_specs=pl.BlockSpec(memory_space=pltpu.VMEM),
-        scratch_shapes=gather_sems(rows),
+        scratch_shapes=gather_sems(rows, cuts),
         compiler_params=pltpu.CompilerParams(
             collective_id=1, has_side_effects=True, vmem_limit_bytes=32 * 1024 * 1024),
         name="gather",
-    )(block).reshape(rows * tiles * part, width)
+    )(block.reshape(cuts, part // cuts, width)).reshape(rows * tiles * part, width)
 
 
 def local(rows, tiles, right_side, diag_inverse, u_factor, v_factor, ranks, pivots):

time: 343 us -> 291 us (0.85)
  Pallas kernels: 265 us -> 214 us
    pallas_call x6, Pallas kernels: 265 us -> 214 us  [the longest x3 144 us: spread(): pl.pallas_call(functools.partial(spread_kernel, rows, cuts), out_shape=ja...]
where the time goes in v2:
time: 291 us; the launch traced here: 290 us
  Pallas kernels  214 us (74%)
  matrix products  32.2 us (11%)
  blocking collectives  16.4 us (6%)
  local copies, waits for them, and re-layouts  10.7 us (4%)
  between operations  10.6 us (4%)
  other arithmetic  5.79 us (2%)
    pallas_call x3, Pallas kernels, spread(): pl.pallas_call(functools.partial(spread_kernel, rows, cuts), out_shape=ja...  144 us
    pallas_call x3, Pallas kernels, gather(): pl.pallas_call(functools.partial(gather_kernel, rows, cuts), out_shape=ja...  69.9 us
    psum x3, blocking collectives, local(): coef = lax.psum(partial_value, 'tile')  16.4 us
    dot_general x3, matrix products, local(): jnp.dot(u_factor[0, step], coef, preferred_element_type=jnp.float32)  15.3 us
    dot_general x3, matrix products, local(): jnp.dot(diag_inverse[step], whole_pivot, preferred_element_type=jnp.float32)  8.67 us
    dot_general x3, matrix products, local(): lax.dot_general(v_factor[0, step], own_unknowns, (((0,), (0,)), ((), ()))...  8.27 us

profile of v2, /device:TPU:0, one launch (start us, length us, event | category | flops | bytes accessed | tf_op | source)
XLA Modules:
  0.0 290.1 jit_solution(1015180591992900973)
XLA Ops:
  0.6 0.0 copy-start
  0.7 1.4 compare_reduce_fusion
  2.0 1.3 compare_reduce_fusion.1
  3.4 1.4 fusion.65
  4.7 0.6 iota_compare_fusion
  5.4 0.7 iota_compare_fusion.2
  6.0 0.6 iota_compare_fusion.1
  6.7 1.4 fusion.66
  17.9 0.1 add_convert_fusion.flags
  18.0 0.1 add_convert_fusion.2.flags
  18.0 0.1 add_convert_fusion.1.flags
  18.1 1.7 copy.8
  19.8 0.0 copy-done
  19.8 49.9 %spread.3 = bf16[2,8,4,64,384]{4,3,2,1,0:T(8,128)(2,1)S(1)} custom-call(f32[5]{0:T(128)S(1)} %add_convert_fusion.flags, bf16[8,256,384]{2,1,0:T(8,128)(2,1)S(1)} %bitcast.100), custom_call_target="tpu_custom_call" | custom-call | tf_op jit(solution)/shard_map/spread/pallas_call | solution.py:240
  69.8 2.9 fusion.43
  72.7 23.6 %gather.3 = bf16[8,2,4,64,384]{4,3,2,1,0:T(8,128)(2,1)S(1)} custom-call(bf16[4,64,384]{2,1,0:T(8,128)(2,1)S(1)} %bitcast.109), custom_call_target="tpu_custom_call" | custom-call | tf_op jit(solution)/shard_map/gather/pallas_call | solution.py:264
  96.3 2.4 fusion.28
  98.7 5.2 %all-reduce.3 = bf16[384,384]{1,0:T(8,128)(2,1)S(1)} all-reduce(f32[384,384]{1,0:T(8,128)S(1)} %fusion.28), channel_id=1, replica_groups=mesh['grp'=2,'row'=8,'tile'=2] {'tile'}, use_global_device_ids=true, to_apply=%region_0.1 | all-reduce | flops 147456 | bytes 884736 | tf_op jit(solution)/shard_map/psum | solution.py:299
  103.9 4.8 %fusion.67 = (bf16[2048,384]{0,1:T(8,128)(2,1)}, f32[2048,384]{0,1:T(8,128)}) fusion(bf16[1,3,2048,384]{3,2,1,0:T(8,128)(2,1)} %param.8, bf16[384,384]{1,0:T(8,128)(2,1)S(1)} %all-reduce.3, pred[384]{0:T(512)(128)(4,1)S(1)} %iota_compare_fusion.2, pred[]{:T(512)} %bitcast.11, bf16[1,2048,384]{1,2,0:T(8,128)(2,1)S(1)} %copy.8), kind=kOutput, calls=%fused_computation.69 | convolution fusion | flops 607272960 | bytes 8160128 | tf_op jit(solution)/shard_map/dot_general | solution.py:301
  108.7 1.9 copy.9
  110.6 47.2 %spread.4 = bf16[2,8,4,64,384]{4,3,2,1,0:T(8,128)(2,1)S(1)} custom-call(f32[5]{0:T(128)S(1)} %add_convert_fusion.1.flags, bf16[8,256,384]{2,1,0:T(8,128)(2,1)S(1)} %bitcast.101), custom_call_target="tpu_custom_call" | custom-call | tf_op jit(solution)/shard_map/spread/pallas_call | solution.py:240
  157.8 2.9 fusion.46
  160.7 22.7 %gather.4 = bf16[8,2,4,64,384]{4,3,2,1,0:T(8,128)(2,1)S(1)} custom-call(bf16[4,64,384]{2,1,0:T(8,128)(2,1)S(1)} %bitcast.111), custom_call_target="tpu_custom_call" | custom-call | tf_op jit(solution)/shard_map/gather/pallas_call | solution.py:264
  183.4 2.4 fusion.33
  185.8 5.3 %all-reduce.4 = bf16[384,384]{1,0:T(8,128)(2,1)S(1)} all-reduce(f32[384,384]{1,0:T(8,128)S(1)} %fusion.33), channel_id=1, replica_groups=mesh['grp'=2,'row'=8,'tile'=2] {'tile'}, use_global_device_ids=true, to_apply=%region_2.3 | all-reduce | flops 147456 | bytes 884736 | tf_op jit(solution)/shard_map/psum | solution.py:299
  191.2 5.8 %fusion.68 = (bf16[2048,384]{0,1:T(8,128)(2,1)S(1)}, f32[2048,384]{0,1:T(8,128)}) fusion(f32[2048,384]{0,1:T(8,128)} %get-tuple-element.11, bf16[1,3,2048,384]{3,2,1,0:T(8,128)(2,1)} %param.8, bf16[384,384]{1,0:T(8,128)(2,1)S(1)} %all-reduce.4, pred[384]{0:T(512)(128)(4,1)S(1)} %iota_compare_fusion.1, pred[]{:T(512)} %compare_reduce_fusion.1), kind=kOutput, calls=%fused_computation.70 | convolution fusion | flops 606486528 | bytes 9732992 | tf_op jit(solution)/shard_map/dot_general | solution.py:301
  197.0 0.9 copy.10
  197.8 47.2 %spread.5 = bf16[2,8,4,64,384]{4,3,2,1,0:T(8,128)(2,1)S(1)} custom-call(f32[5]{0:T(128)S(1)} %add_convert_fusion.2.flags, bf16[8,256,384]{2,1,0:T(8,128)(2,1)S(1)} %bitcast.102), custom_call_target="tpu_custom_call" | custom-call | tf_op jit(solution)/shard_map/spread/pallas_call | solution.py:240
  245.0 2.9 fusion.49
  247.9 0.9 pad_maximum_fusion
  248.8 23.5 %gather.5 = bf16[8,2,4,64,384]{4,3,2,1,0:T(8,128)(2,1)S(1)} custom-call(bf16[4,64,384]{2,1,0:T(8,128)(2,1)S(1)} %bitcast.114), custom_call_target="tpu_custom_call" | custom-call | tf_op jit(solution)/shard_map/gather/pallas_call | solution.py:264
  272.4 0.0 copy-start.1
  272.4 3.4 %fusion.38 = f32[384,384]{1,0:T(8,128)} fusion(bf16[1,3,2048,384]{3,2,1,0:T(8,128)(2,1)} %param.9, bf16[4096,384]{1,0:T(8,128)(2,1)S(1)} %bitcast.105, s32[]{:T(128)S(6)} %select_n.64), kind=kOutput, calls=%fused_computation.33 | convolution fusion | flops 603979776 | bytes 3735556 | tf_op jit(solution)/shard_map/dot_general | solution.py:293
  275.8 5.9 %all-reduce.5 = bf16[384,384]{1,0:T(8,128)(2,1)S(1)} all-reduce(f32[384,384]{1,0:T(8,128)} %fusion.38), channel_id=1, replica_groups=mesh['grp'=2,'row'=8,'tile'=2] {'tile'}, use_global_device_ids=true, to_apply=%region_4.5 | all-reduce | flops 147456 | bytes 884736 | tf_op jit(solution)/shard_map/psum | solution.py:299
  281.7 0.0 copy-done.1
  281.8 4.8 %fusion = f32[1,2048,384]{1,2,0:T(8,128)} fusion(f32[2048,384]{0,1:T(8,128)S(1)} %copy-done.1, bf16[1,3,2048,384]{3,2,1,0:T(8,128)(2,1)} %param.8, pred[]{:T(512)} %compare_reduce_fusion, bf16[384,384]{1,0:T(8,128)(2,1)S(1)} %all-reduce.5, pred[384]{0:T(512)(128)(4,1)S(1)} %iota_compare_fusion), kind=kOutput, calls=%fused_computation.2 | convolution fusion | flops 605700096 | bytes 8160128 | tf_op jit(solution)/shard_map/dot_general | solution.py:301
  286.5 3.5 %copy.11 = f32[1,2048,384]{2,1,0:T(8,128)} copy(f32[1,2048,384]{1,2,0:T(8,128)} %fusion) | data formatting | bytes 6291456
  (2 shorter events, 0.0 us)
Async XLA Ops:
  0.6 19.2 %copy-start = (bf16[1,2048,384]{2,1,0:T(8,128)(2,1)S(1)}, bf16[1,2048,384]{2,1,0:T(8,128)(2,1)}, u32[]{:S(2)}) copy-start(bf16[1,2048,384]{2,1,0:T(8,128)(2,1)} %param.6) | copy-start | bytes 4718596
  272.4 9.4 %copy-start.1 = (f32[2048,384]{0,1:T(8,128)S(1)}, f32[2048,384]{0,1:T(8,128)}, u32[]{:S(2)}) copy-start(f32[2048,384]{0,1:T(8,128)} %get-tuple-element.13) | copy-start | bytes 9437188

commit v3 on v2

--- a/solution.py
+++ b/solution.py
@@ -181,13 +181,77 @@
     return [column] * 5 + [whole] * 2
 
 
-def gather_kernel(rows, cuts, src, out, *sems):
+def indicator(condition):
+    return jnp.where(condition, jnp.float32(1.0), jnp.float32(0.0))
+
+
+def solve_kernel(rows, cuts, step, pivots, ranks, pivot_block, diag, u_hbm, v_hbm, residual,
+                 solved, new_residual, current, diag_buf, u_buf, v_buf, res_buf, total, piece, full,
+                 partial, other, load_sems, mate_send, mate_recv, *sems):
     at = Place(rows)
+    part, width = solved.shape
+    loads = [
+        pltpu.make_async_copy(diag.at[step], diag_buf, load_sems.at[0]),
+        pltpu.make_async_copy(v_hbm.at[0, step], v_buf, load_sems.at[1]),
+        pltpu.make_async_copy(u_hbm.at[0, step], u_buf, load_sems.at[2]),
+        pltpu.make_async_copy(residual, res_buf, load_sems.at[3]),
+    ]
+    for load in loads:
+        load.start()
     greet(at)
-    gather_body(at, cuts, src, lambda row, tile, cut: out.at[row, tile, cut], sems)
-
-
-def spread_kernel(rows, cuts, flags, src, out, from_side, mixed, from_col, piece,
+    loads[0].wait()
+    depth = diag_buf.shape[1]
+    span = depth // 8
+    total[...] = jnp.zeros_like(total)
+
+    def product(i):
+        k = pl.multiple_of(i * span, span)
+        total[...] += jnp.dot(diag_buf[:, pl.ds(k, span)], pivot_block[pl.ds(k, span), :],
+                              preferred_element_type=jnp.float32)
+
+    each(0, 8, product)
+    own = total[...].astype(jnp.bfloat16)
+    solved[...] = own
+    piece[...] = own.reshape(piece.shape)
+    gather_body(at, cuts, piece, lambda row, tile, cut: full.at[row, tile, cut], sems)
+    loads[1].wait()
+    partial[...] = jnp.zeros_like(partial)
+    lanes = at.lanes
+
+    def inner(i):
+        k = pl.multiple_of(i * part, part)
+        values = full[at.tile * lanes + lax.div(i, 2), lax.rem(i, 2)].reshape(part, width)
+        partial[...] += lax.dot_general(v_buf[pl.ds(k, part), :], values, (((0,), (0,)), ((), ())),
+                                        preferred_element_type=jnp.float32)
+
+    each(0, rows, inner)
+    swap = pltpu.make_async_remote_copy(
+        src_ref=partial, dst_ref=other, send_sem=mate_send, recv_sem=mate_recv,
+        device_id=at.to(at.row, 1 - at.tile), device_id_type=MESH)
+    swap.start()
+    loads[2].wait()
+    loads[3].wait()
+    swap.wait()
+    columns = lax.broadcasted_iota(jnp.int32, partial.shape, 0)
+    coef = jnp.where(columns < ranks[0, step], partial[...] + other[...], jnp.float32(0.0))
+    coef = coef.astype(jnp.bfloat16)
+    keep = jnp.float32(1.0)
+    for p in range(step + 1):
+        keep = keep * indicator(pivots[p] != at.row)
+    height = res_buf.shape[0]
+    block = height // 8
+
+    def outer(i):
+        k = pl.ds(pl.multiple_of(i * block, block), block)
+        update = jnp.dot(u_buf[k, :], coef, preferred_element_type=jnp.float32)
+        value = res_buf[k, :] - update * keep
+        new_residual[k, :] = value
+        current[k, :] = value.astype(jnp.bfloat16)
+
+    each(0, 8, outer)
+
+
+def spread_kernel(rows, cuts, step, pivots, src, out, from_side, mixed, from_col, piece,
                   rs_sends, rs_side, rs_col, *sems):
     at = Place(rows)
     lanes = at.lanes
@@ -202,7 +266,9 @@
             device_id=at.to(side_row, at.tile), device_id_type=MESH)
         copy.start()
         side_copies[k] = copy
-    own = flags[0]
+    root = pivots[step]
+    own = indicator(root == at.row)
+    root_lane = lax.div(root, 2)
     col_copies = {}
     for k in order:
         side_copies[k].wait_recv()
@@ -216,10 +282,10 @@
                 device_id=at.to(at.peer(k), at.tile), device_id_type=MESH)
             copy.start()
             col_copies[k] = copy
-    total = mixed[0].astype(jnp.float32) * flags[1]
+    total = mixed[0].astype(jnp.float32) * indicator(root_lane == at.lane)
     for k in range(1, lanes):
         col_copies[k].wait_recv()
-        total = total + from_col[k].astype(jnp.float32) * flags[1 + k]
+        total = total + from_col[k].astype(jnp.float32) * indicator(root_lane == lax.div(at.source(k), 2))
     piece[...] = total.astype(jnp.bfloat16).reshape(piece.shape)
     for k in order:
         side_copies[k].wait_send()
@@ -228,17 +294,13 @@
     gather_body(at, cuts, piece, lambda row, tile, cut: out.at[tile, row, cut], sems)
 
 
-def spread(rows, tiles, current, root):
+def spread(rows, tiles, step, current, pivots):
     half, width = current.shape
     part = half // rows
     lanes = rows // 2
     cuts = cuts_of(part)
-    me = lax.axis_index("row")
-    lane = me // 2
-    sources = lax.rem(lane + lanes - jnp.arange(lanes, dtype=jnp.int32), lanes)
-    flags = jnp.concatenate([(root == me)[None], sources == root // 2]).astype(jnp.float32)
     out = pl.pallas_call(
-        functools.partial(spread_kernel, rows, cuts),
+        functools.partial(spread_kernel, rows, cuts, step),
         out_shape=jax.ShapeDtypeStruct((tiles, rows, cuts, part // cuts, width), jnp.bfloat16),
         in_specs=[pl.BlockSpec(memory_space=pltpu.SMEM), pl.BlockSpec(memory_space=pltpu.VMEM)],
         out_specs=pl.BlockSpec(memory_space=pltpu.VMEM),
@@ -252,55 +314,58 @@
             pltpu.SemaphoreType.DMA((lanes,)),
         ] + gather_sems(rows, cuts),
         compiler_params=pltpu.CompilerParams(
-            collective_id=0, has_side_effects=True, vmem_limit_bytes=32 * 1024 * 1024),
+            collective_id=2 * step, has_side_effects=True, vmem_limit_bytes=32 * 1024 * 1024),
         name="spread",
-    )(flags, current.reshape(rows, part, width))
+    )(pivots, current.reshape(rows, part, width))
     return out.reshape(tiles * half, width)
 
 
-def gather(rows, tiles, block):
-    part, width = block.shape
+def solve(rows, tiles, step, pivots, ranks, pivot_block, diag, u_factor, v_factor, residual):
+    part, depth = diag.shape[1:]
+    height, width = residual.shape
+    rank_width = u_factor.shape[3]
     cuts = cuts_of(part)
+    smem = pl.BlockSpec(memory_space=pltpu.SMEM)
+    vmem = pl.BlockSpec(memory_space=pltpu.VMEM)
+    anywhere = pl.BlockSpec(memory_space=pl.ANY)
     return pl.pallas_call(
-        functools.partial(gather_kernel, rows, cuts),
-        out_shape=jax.ShapeDtypeStruct((rows, tiles, cuts, part // cuts, width), jnp.bfloat16),
-        in_specs=[pl.BlockSpec(memory_space=pltpu.VMEM)],
-        out_specs=pl.BlockSpec(memory_space=pltpu.VMEM),
-        scratch_shapes=gather_sems(rows, cuts),
+        functools.partial(solve_kernel, rows, cuts, step),
+        out_shape=(
+            jax.ShapeDtypeStruct((part, width), jnp.bfloat16),
+            jax.ShapeDtypeStruct((height, width), jnp.float32),
+            jax.ShapeDtypeStruct((height, width), jnp.bfloat16),
+        ),
+        in_specs=[smem, smem, vmem, anywhere, anywhere, anywhere, anywhere],
+        out_specs=(vmem, vmem, vmem),
+        scratch_shapes=[
+            pltpu.VMEM((part, depth), jnp.bfloat16),
+            pltpu.VMEM((height, rank_width), jnp.bfloat16),
+            pltpu.VMEM((height, rank_width), jnp.bfloat16),
+            pltpu.VMEM((height, width), jnp.float32),
+            pltpu.VMEM((part, width), jnp.float32),
+            pltpu.VMEM((cuts, part // cuts, width), jnp.bfloat16),
+            pltpu.VMEM((rows, tiles, cuts, part // cuts, width), jnp.bfloat16),
+            pltpu.VMEM((rank_width, width), jnp.float32),
+            pltpu.VMEM((rank_width, width), jnp.float32),
+            pltpu.SemaphoreType.DMA((4,)),
+            pltpu.SemaphoreType.DMA,
+            pltpu.SemaphoreType.DMA,
+        ] + gather_sems(rows, cuts),
         compiler_params=pltpu.CompilerParams(
-            collective_id=1, has_side_effects=True, vmem_limit_bytes=32 * 1024 * 1024),
-        name="gather",
-    )(block.reshape(cuts, part // cuts, width)).reshape(rows * tiles * part, width)
+            collective_id=2 * step + 1, has_side_effects=True, vmem_limit_bytes=40 * 1024 * 1024),
+        name="solve",
+    )(pivots, ranks, pivot_block, diag, u_factor, v_factor, residual)
 
 
 def local(rows, tiles, right_side, diag_inverse, u_factor, v_factor, ranks, pivots):
-    residual = right_side[0].astype(jnp.float32)
-    half_rows = residual.shape[0]
-    rank_width = u_factor.shape[3]
-    columns = lax.broadcasted_iota(jnp.int32, (rank_width, 1), 0)
-    my_block = lax.axis_index("row")
-    tile_at = lax.axis_index("tile")
+    current = right_side[0]
+    residual = current.astype(jnp.float32)
     solved_list = []
     for step in range(PIVOTS):
-        current = residual.astype(jnp.bfloat16)
-        whole_pivot = spread(rows, tiles, current, pivots[step])
-        part_unknowns = jnp.dot(
-            diag_inverse[step], whole_pivot, preferred_element_type=jnp.float32
-        ).astype(jnp.bfloat16)
-        solved_list.append(part_unknowns)
-        full_unknowns = gather(rows, tiles, part_unknowns)
-        own_unknowns = lax.dynamic_slice_in_dim(full_unknowns, tile_at * half_rows, half_rows, 0)
-        partial_value = lax.dot_general(
-            v_factor[0, step],
-            own_unknowns,
-            (((0,), (0,)), ((), ())),
-            preferred_element_type=jnp.float32,
-        )
-        coef = lax.psum(partial_value, "tile")
-        coef = jnp.where(columns < ranks[0, step], coef, jnp.float32(0.0)).astype(jnp.bfloat16)
-        update = jnp.dot(u_factor[0, step], coef, preferred_element_type=jnp.float32)
-        finished = jnp.any(pivots[: step + 1] == my_block)
-        residual = residual - jnp.where(finished, jnp.float32(0.0), update)
+        pivot_block = spread(rows, tiles, step, current, pivots)
+        solved, residual, current = solve(
+            rows, tiles, step, pivots, ranks, pivot_block, diag_inverse, u_factor, v_factor, residual)
+        solved_list.append(solved)
     return (jnp.stack(solved_list), residual[None])
 
 

time: 291 us -> 251 us (0.86)
  matrix products: 32.2 us -> 0 us
  Pallas kernels: 214 us -> 245 us
  blocking collectives: 16.4 us -> 0 us
  between operations: 10.6 us -> 0.71 us
  local copies, waits for them, and re-layouts: 10.7 us -> 4.16 us
  other arithmetic: 5.79 us -> 1.1 us
    dot_general x9 -> x0, matrix products: 32.2 us -> none  [the longest x3 15.3 us: local(): jnp.dot(u_factor[0, step], coef, preferred_element_type=jnp.float32)]
    pallas_call x6, Pallas kernels: 214 us -> 245 us  [the longest x3 144 us: spread(): pl.pallas_call(functools.partial(spread_kernel, rows, cuts, step), out_sh...]
    psum x3 -> x0, blocking collectives: 16.4 us -> none  [local(): coef = lax.psum(partial_value, 'tile')]
where the time goes in v3:
time: 251 us
  Pallas kernels  245 us (98%)
  local copies, waits for them, and re-layouts  4.16 us (2%)
    pallas_call x3, Pallas kernels, spread(): pl.pallas_call(functools.partial(spread_kernel, rows, cuts, step), out_sh...  144 us
    pallas_call x3, Pallas kernels, solve(): pl.pallas_call(functools.partial(solve_kernel, rows, cuts, step), out_sha...  100 us

profile of v3, /device:TPU:0, one launch (start us, length us, event | category | flops | bytes accessed | tf_op | source)
XLA Modules:
  0.0 250.6 jit_solution(7238314338524595173)
XLA Ops:
  0.6 0.0 copy-start
  0.6 1.4 copy-done
  2.0 0.0 copy-start.1
  2.0 0.7 copy-done.1
  2.7 49.9 %spread.3 = bf16[2,8,4,64,384]{4,3,2,1,0:T(8,128)(2,1)S(1)} custom-call(s32[3]{0:T(128)S(1)} %copy-done.1, bf16[8,256,384]{2,1,0:T(8,128)(2,1)S(1)} %bitcast.16), custom_call_target="tpu_custom_call" | custom-call | tf_op jit(solution)/shard_map/spread/pallas_call | solution.py:302
  52.6 0.0 copy-start.2
  52.6 0.0 copy-start.3
  52.6 0.2 bitcast_convert_fusion.residual
  52.9 0.4 copy-done.2
  53.3 0.0 copy-done.3
  53.3 33.3 %solve.3 = (bf16[256,384]{1,0:T(8,128)(2,1)S(1)}, f32[2048,384]{1,0:T(8,128)S(1)}, bf16[2048,384]{1,0:T(8,128)(2,1)S(1)}) custom-call(s32[3]{0:T(128)S(1)} %copy-done.2, s32[1,3]{1,0:T(1,128)S(1)} %copy-done.3, bf16[4096,384]{1,0:T(8,128)(2,1)S(1)} %bitcast.15, bf16[3,256,4096]{2,1,0:T(8,128)(2,1)} %diag.5, bf16[1,3,2048,384]{3,2,1,0:T(8,128)(2,1)} %u_hbm.5, ...), custom_call_target="tpu_custom_call" | custom-call | tf_op jit(solution)/shard_map/solve/pallas_call | solution.py:331
  86.6 47.2 %spread.4 = bf16[2,8,4,64,384]{4,3,2,1,0:T(8,128)(2,1)S(1)} custom-call(s32[3]{0:T(128)S(1)} %copy-done.2, bf16[8,256,384]{2,1,0:T(8,128)(2,1)S(1)} %bitcast.18), custom_call_target="tpu_custom_call" | custom-call | tf_op jit(solution)/shard_map/spread/pallas_call | solution.py:302
  133.8 32.5 %solve.4 = (bf16[256,384]{1,0:T(8,128)(2,1)S(1)}, f32[2048,384]{1,0:T(8,128)S(1)}, bf16[2048,384]{1,0:T(8,128)(2,1)S(1)}) custom-call(s32[3]{0:T(128)S(1)} %copy-done.2, s32[1,3]{1,0:T(1,128)S(1)} %copy-done.3, bf16[4096,384]{1,0:T(8,128)(2,1)S(1)} %bitcast.13, bf16[3,256,4096]{2,1,0:T(8,128)(2,1)} %diag.5, bf16[1,3,2048,384]{3,2,1,0:T(8,128)(2,1)} %u_hbm.5, ...), custom_call_target="tpu_custom_call" | custom-call | tf_op jit(solution)/shard_map/solve/pallas_call | solution.py:331
  166.3 47.3 %spread.5 = bf16[2,8,4,64,384]{4,3,2,1,0:T(8,128)(2,1)S(1)} custom-call(s32[3]{0:T(128)S(1)} %copy-done.2, bf16[8,256,384]{2,1,0:T(8,128)(2,1)S(1)} %bitcast.19), custom_call_target="tpu_custom_call" | custom-call | tf_op jit(solution)/shard_map/spread/pallas_call | solution.py:302
  213.6 34.4 %solve.5 = (bf16[256,384]{1,0:T(8,128)(2,1)S(1)}, f32[2048,384]{1,0:T(8,128)S(1)}, bf16[2048,384]{1,0:T(8,128)(2,1)}) custom-call(s32[3]{0:T(128)S(1)} %copy-done.2, s32[1,3]{1,0:T(1,128)S(1)} %copy-done.3, bf16[4096,384]{1,0:T(8,128)(2,1)S(1)} %bitcast.14, bf16[3,256,4096]{2,1,0:T(8,128)(2,1)} %diag.5, bf16[1,3,2048,384]{3,2,1,0:T(8,128)(2,1)} %u_hbm.5, ...), custom_call_target="tpu_custom_call" | custom-call | tf_op jit(solution)/shard_map/solve/pallas_call | solution.py:331
  248.0 0.9 pad_maximum_fusion
  248.9 1.7 copy.9
Async XLA Ops:
  0.6 1.4 copy-start
  2.0 0.7 copy-start.1
  52.6 0.7 copy-start.2
  52.6 0.7 copy-start.3

commit v4 on v3

--- a/solution.py
+++ b/solution.py
@@ -51,7 +51,7 @@
     lax.fori_loop(low, high, step, 0)
 
 
-def gather_body(at, cuts, src, out_at, sems):
+def gather_body(at, cuts, src, out_at, sems, ready=None):
     z_right, z_left, z_recv, x_send, x_recv, t_send, t_recv = sems
     lane, last = at.lane, at.lanes - 1
     side_row = at.across(at.row)
@@ -88,6 +88,9 @@
         copy(slot, slot, t_send.at[0], sem, at.to(at.row, mate)).wait_recv()
 
     for cut in range(cuts):
+        if ready is not None:
+            ready(cut)
+
         @pl.when(lane < last)
         def _(cut=cut):
             right(src.at[cut], lane, cut).start()
@@ -259,39 +262,51 @@
     side_row = at.across(at.row)
     order = list(range(1, lanes)) + [0]
     side_copies = {}
-    for k in order:
-        copy = pltpu.make_async_remote_copy(
-            src_ref=src.at[at.across(at.peer(k))], dst_ref=from_side.at[k],
-            send_sem=rs_sends.at[k], recv_sem=rs_side.at[k],
-            device_id=at.to(side_row, at.tile), device_id_type=MESH)
-        copy.start()
-        side_copies[k] = copy
+    for cut in range(cuts):
+        for k in order:
+            i = cut * lanes + k
+            copy = pltpu.make_async_remote_copy(
+                src_ref=src.at[at.across(at.peer(k)), cut], dst_ref=from_side.at[i],
+                send_sem=rs_sends.at[i], recv_sem=rs_side.at[i],
+                device_id=at.to(side_row, at.tile), device_id_type=MESH)
+            copy.start()
+            side_copies[i] = copy
     root = pivots[step]
     own = indicator(root == at.row)
     root_lane = lax.div(root, 2)
     col_copies = {}
-    for k in order:
-        side_copies[k].wait_recv()
-        value = src[at.peer(k)].astype(jnp.float32) * own
-        value = value + from_side[k].astype(jnp.float32) * (1.0 - own)
-        mixed[k] = value.astype(jnp.bfloat16)
-        if k:
-            copy = pltpu.make_async_remote_copy(
-                src_ref=mixed.at[k], dst_ref=from_col.at[k],
-                send_sem=rs_sends.at[lanes + k], recv_sem=rs_col.at[k],
-                device_id=at.to(at.peer(k), at.tile), device_id_type=MESH)
-            copy.start()
-            col_copies[k] = copy
-    total = mixed[0].astype(jnp.float32) * indicator(root_lane == at.lane)
-    for k in range(1, lanes):
-        col_copies[k].wait_recv()
-        total = total + from_col[k].astype(jnp.float32) * indicator(root_lane == lax.div(at.source(k), 2))
-    piece[...] = total.astype(jnp.bfloat16).reshape(piece.shape)
-    for k in order:
-        side_copies[k].wait_send()
-        if k:
-            col_copies[k].wait_send()
-    gather_body(at, cuts, piece, lambda row, tile, cut: out.at[tile, row, cut], sems)
+
+    def mix(cut):
+        for k in order:
+            i = cut * lanes + k
+            side_copies[i].wait_recv()
+            value = src[at.peer(k), cut].astype(jnp.float32) * own
+            value = value + from_side[i].astype(jnp.float32) * (1.0 - own)
+            mixed[i] = value.astype(jnp.bfloat16)
+            if k:
+                copy = pltpu.make_async_remote_copy(
+                    src_ref=mixed.at[i], dst_ref=from_col.at[i],
+                    send_sem=rs_sends.at[cuts * lanes + i], recv_sem=rs_col.at[i],
+                    device_id=at.to(at.peer(k), at.tile), device_id_type=MESH)
+                copy.start()
+                col_copies[i] = copy
+
+    def ready(cut):
+        if cut == 0:
+            mix(0)
+        if cut + 1 < cuts:
+            mix(cut + 1)
+        total = mixed[cut * lanes].astype(jnp.float32) * indicator(root_lane == at.lane)
+        for k in range(1, lanes):
+            i = cut * lanes + k
+            col_copies[i].wait_recv()
+            total = total + from_col[i].astype(jnp.float32) * indicator(
+                root_lane == lax.div(at.source(k), 2))
+        piece[cut] = total.astype(jnp.bfloat16)
+
+    gather_body(at, cuts, piece, lambda row, tile, cut: out.at[tile, row, cut], sems, ready)
+    for copy in list(side_copies.values()) + list(col_copies.values()):
+        copy.wait_send()
 
 
 def spread(rows, tiles, step, current, pivots):
@@ -305,18 +320,18 @@
         in_specs=[pl.BlockSpec(memory_space=pltpu.SMEM), pl.BlockSpec(memory_space=pltpu.VMEM)],
         out_specs=pl.BlockSpec(memory_space=pltpu.VMEM),
         scratch_shapes=[
-            pltpu.VMEM((lanes, part, width), jnp.bfloat16),
-            pltpu.VMEM((lanes, part, width), jnp.bfloat16),
-            pltpu.VMEM((lanes, part, width), jnp.bfloat16),
+            pltpu.VMEM((cuts * lanes, part // cuts, width), jnp.bfloat16),
+            pltpu.VMEM((cuts * lanes, part // cuts, width), jnp.bfloat16),
+            pltpu.VMEM((cuts * lanes, part // cuts, width), jnp.bfloat16),
             pltpu.VMEM((cuts, part // cuts, width), jnp.bfloat16),
-            pltpu.SemaphoreType.DMA((2 * lanes,)),
-            pltpu.SemaphoreType.DMA((lanes,)),
-            pltpu.SemaphoreType.DMA((lanes,)),
+            pltpu.SemaphoreType.DMA((2 * cuts * lanes,)),
+            pltpu.SemaphoreType.DMA((cuts * lanes,)),
+            pltpu.SemaphoreType.DMA((cuts * lanes,)),
         ] + gather_sems(rows, cuts),
         compiler_params=pltpu.CompilerParams(
             collective_id=2 * step, has_side_effects=True, vmem_limit_bytes=32 * 1024 * 1024),
         name="spread",
-    )(pivots, current.reshape(rows, part, width))
+    )(pivots, current.reshape(rows, cuts, part // cuts, width))
     return out.reshape(tiles * half, width)
 
 

time: 251 us -> 240 us (0.956)
  Pallas kernels: 245 us -> 234 us
    pallas_call x3, Pallas kernels: 144 us -> 133 us  [spread(): pl.pallas_call(functools.partial(spread_kernel, rows, cuts, step), out_sh...]
where the time goes in v4:
time: 240 us
  Pallas kernels  234 us (98%)
  local copies, waits for them, and re-layouts  4.16 us (2%)
    pallas_call x3, Pallas kernels, spread(): pl.pallas_call(functools.partial(spread_kernel, rows, cuts, step), out_sh...  133 us
    pallas_call x3, Pallas kernels, solve(): pl.pallas_call(functools.partial(solve_kernel, rows, cuts, step), out_sha...  101 us

profile of v4, /device:TPU:0, one launch (start us, length us, event | category | flops | bytes accessed | tf_op | source)
XLA Modules:
  0.0 240.1 jit_solution(3227633094459574696)
XLA Ops:
  0.6 0.0 copy-start
  0.6 1.4 copy-done
  2.0 0.0 copy-start.1
  2.0 0.7 copy-done.1
  2.7 46.3 %spread.3 = bf16[2,8,4,64,384]{4,3,2,1,0:T(8,128)(2,1)S(1)} custom-call(s32[3]{0:T(128)S(1)} %copy-done.1, bf16[8,4,64,384]{3,2,1,0:T(8,128)(2,1)S(1)} %bitcast.16), custom_call_target="tpu_custom_call" | custom-call | tf_op jit(solution)/shard_map/spread/pallas_call | solution.py:317
  49.0 0.0 copy-start.2
  49.0 0.0 copy-start.3
  49.0 0.2 bitcast_convert_fusion.residual
  49.2 0.4 copy-done.2
  49.6 0.0 copy-done.3
  49.6 33.4 %solve.3 = (bf16[256,384]{1,0:T(8,128)(2,1)S(1)}, f32[2048,384]{1,0:T(8,128)S(1)}, bf16[2048,384]{1,0:T(8,128)(2,1)S(1)}) custom-call(s32[3]{0:T(128)S(1)} %copy-done.2, s32[1,3]{1,0:T(1,128)S(1)} %copy-done.3, bf16[4096,384]{1,0:T(8,128)(2,1)S(1)} %bitcast.15, bf16[3,256,4096]{2,1,0:T(8,128)(2,1)} %diag.5, bf16[1,3,2048,384]{3,2,1,0:T(8,128)(2,1)} %u_hbm.5, ...), custom_call_target="tpu_custom_call" | custom-call | tf_op jit(solution)/shard_map/solve/pallas_call | solution.py:346
  83.1 43.4 %spread.4 = bf16[2,8,4,64,384]{4,3,2,1,0:T(8,128)(2,1)S(1)} custom-call(s32[3]{0:T(128)S(1)} %copy-done.2, bf16[8,4,64,384]{3,2,1,0:T(8,128)(2,1)S(1)} %bitcast.18), custom_call_target="tpu_custom_call" | custom-call | tf_op jit(solution)/shard_map/spread/pallas_call | solution.py:317
  126.5 32.7 %solve.4 = (bf16[256,384]{1,0:T(8,128)(2,1)S(1)}, f32[2048,384]{1,0:T(8,128)S(1)}, bf16[2048,384]{1,0:T(8,128)(2,1)S(1)}) custom-call(s32[3]{0:T(128)S(1)} %copy-done.2, s32[1,3]{1,0:T(1,128)S(1)} %copy-done.3, bf16[4096,384]{1,0:T(8,128)(2,1)S(1)} %bitcast.13, bf16[3,256,4096]{2,1,0:T(8,128)(2,1)} %diag.5, bf16[1,3,2048,384]{3,2,1,0:T(8,128)(2,1)} %u_hbm.5, ...), custom_call_target="tpu_custom_call" | custom-call | tf_op jit(solution)/shard_map/solve/pallas_call | solution.py:346
  159.2 43.5 %spread.5 = bf16[2,8,4,64,384]{4,3,2,1,0:T(8,128)(2,1)S(1)} custom-call(s32[3]{0:T(128)S(1)} %copy-done.2, bf16[8,4,64,384]{3,2,1,0:T(8,128)(2,1)S(1)} %bitcast.19), custom_call_target="tpu_custom_call" | custom-call | tf_op jit(solution)/shard_map/spread/pallas_call | solution.py:317
  202.7 34.8 %solve.5 = (bf16[256,384]{1,0:T(8,128)(2,1)S(1)}, f32[2048,384]{1,0:T(8,128)S(1)}, bf16[2048,384]{1,0:T(8,128)(2,1)}) custom-call(s32[3]{0:T(128)S(1)} %copy-done.2, s32[1,3]{1,0:T(1,128)S(1)} %copy-done.3, bf16[4096,384]{1,0:T(8,128)(2,1)S(1)} %bitcast.14, bf16[3,256,4096]{2,1,0:T(8,128)(2,1)} %diag.5, bf16[1,3,2048,384]{3,2,1,0:T(8,128)(2,1)} %u_hbm.5, ...), custom_call_target="tpu_custom_call" | custom-call | tf_op jit(solution)/shard_map/solve/pallas_call | solution.py:346
  237.5 0.9 pad_maximum_fusion
  238.4 1.7 copy.9
Async XLA Ops:
  0.6 1.4 copy-start
  2.0 0.7 copy-start.1
  49.0 0.7 copy-start.2
  49.0 0.7 copy-start.3

commit v5 on v4

--- a/solution.py
+++ b/solution.py
@@ -175,7 +175,7 @@
 
 
 def cuts_of(part):
-    return max(1, min(4, part // 16))
+    return max(1, min(8, part // 16))
 
 
 def gather_sems(rows, cuts):

time: 240 us -> 252 us (1.050)
  Pallas kernels: 234 us -> 246 us
    pallas_call x3, Pallas kernels: 133 us -> 140 us  [spread(): pl.pallas_call(functools.partial(spread_kernel, rows, cuts, step), out_sh...]
    pallas_call x3, Pallas kernels: 101 us -> 105 us  [solve(): pl.pallas_call(functools.partial(solve_kernel, rows, cuts, step), out_sha...]
where the time goes in v5:
time: 252 us
  Pallas kernels  246 us (98%)
  local copies, waits for them, and re-layouts  4.16 us (2%)
    pallas_call x3, Pallas kernels, spread(): pl.pallas_call(functools.partial(spread_kernel, rows, cuts, step), out_sh...  140 us
    pallas_call x3, Pallas kernels, solve(): pl.pallas_call(functools.partial(solve_kernel, rows, cuts, step), out_sha...  105 us

profile of v5, /device:TPU:0, one launch (start us, length us, event | category | flops | bytes accessed | tf_op | source)
XLA Modules:
  0.0 251.7 jit_solution(17051437098086002018)
XLA Ops:
  0.6 0.0 copy-start
  0.6 1.4 copy-done
  2.0 0.0 copy-start.1
  2.0 0.7 copy-done.1
  2.7 48.0 %spread.3 = bf16[2,8,8,32,384]{4,3,2,1,0:T(8,128)(2,1)S(1)} custom-call(s32[3]{0:T(128)S(1)} %copy-done.1, bf16[8,8,32,384]{3,2,1,0:T(8,128)(2,1)S(1)} %bitcast.16), custom_call_target="tpu_custom_call" | custom-call | tf_op jit(solution)/shard_map/spread/pallas_call | solution.py:317
  50.7 0.0 copy-start.2
  50.7 0.0 copy-start.3
  50.7 0.2 bitcast_convert_fusion.residual
  50.9 0.4 copy-done.2
  51.4 0.0 copy-done.3
  51.4 35.1 %solve.3 = (bf16[256,384]{1,0:T(8,128)(2,1)S(1)}, f32[2048,384]{1,0:T(8,128)S(1)}, bf16[2048,384]{1,0:T(8,128)(2,1)S(1)}) custom-call(s32[3]{0:T(128)S(1)} %copy-done.2, s32[1,3]{1,0:T(1,128)S(1)} %copy-done.3, bf16[4096,384]{1,0:T(8,128)(2,1)S(1)} %bitcast.15, bf16[3,256,4096]{2,1,0:T(8,128)(2,1)} %diag.5, bf16[1,3,2048,384]{3,2,1,0:T(8,128)(2,1)} %u_hbm.5, ...), custom_call_target="tpu_custom_call" | custom-call | tf_op jit(solution)/shard_map/solve/pallas_call | solution.py:346
  86.5 46.2 %spread.4 = bf16[2,8,8,32,384]{4,3,2,1,0:T(8,128)(2,1)S(1)} custom-call(s32[3]{0:T(128)S(1)} %copy-done.2, bf16[8,8,32,384]{3,2,1,0:T(8,128)(2,1)S(1)} %bitcast.18), custom_call_target="tpu_custom_call" | custom-call | tf_op jit(solution)/shard_map/spread/pallas_call | solution.py:317
  132.7 34.0 %solve.4 = (bf16[256,384]{1,0:T(8,128)(2,1)S(1)}, f32[2048,384]{1,0:T(8,128)S(1)}, bf16[2048,384]{1,0:T(8,128)(2,1)S(1)}) custom-call(s32[3]{0:T(128)S(1)} %copy-done.2, s32[1,3]{1,0:T(1,128)S(1)} %copy-done.3, bf16[4096,384]{1,0:T(8,128)(2,1)S(1)} %bitcast.13, bf16[3,256,4096]{2,1,0:T(8,128)(2,1)} %diag.5, bf16[1,3,2048,384]{3,2,1,0:T(8,128)(2,1)} %u_hbm.5, ...), custom_call_target="tpu_custom_call" | custom-call | tf_op jit(solution)/shard_map/solve/pallas_call | solution.py:346
  166.7 46.2 %spread.5 = bf16[2,8,8,32,384]{4,3,2,1,0:T(8,128)(2,1)S(1)} custom-call(s32[3]{0:T(128)S(1)} %copy-done.2, bf16[8,8,32,384]{3,2,1,0:T(8,128)(2,1)S(1)} %bitcast.19), custom_call_target="tpu_custom_call" | custom-call | tf_op jit(solution)/shard_map/spread/pallas_call | solution.py:317
  212.9 36.2 %solve.5 = (bf16[256,384]{1,0:T(8,128)(2,1)S(1)}, f32[2048,384]{1,0:T(8,128)S(1)}, bf16[2048,384]{1,0:T(8,128)(2,1)}) custom-call(s32[3]{0:T(128)S(1)} %copy-done.2, s32[1,3]{1,0:T(1,128)S(1)} %copy-done.3, bf16[4096,384]{1,0:T(8,128)(2,1)S(1)} %bitcast.14, bf16[3,256,4096]{2,1,0:T(8,128)(2,1)} %diag.5, bf16[1,3,2048,384]{3,2,1,0:T(8,128)(2,1)} %u_hbm.5, ...), custom_call_target="tpu_custom_call" | custom-call | tf_op jit(solution)/shard_map/solve/pallas_call | solution.py:346
  249.1 0.9 pad_maximum_fusion
  250.0 1.7 copy.9
Async XLA Ops:
  0.6 1.4 copy-start
  2.0 0.7 copy-start.1
  50.7 0.7 copy-start.2
  50.7 0.7 copy-start.3
